TPU v7x, 256 devices: a whole 4x4x8 slice. The times are simulated.
256 devices in a mesh: lat: 16 (over y_lo, x, core), lon: 16 (over y_hi, z).
Axes of the slice: x: 4, y: 4 (y_hi: 2, y_lo: 2; y = y_hi * 2 + y_lo), z: 8, core: 2. Of those that a mesh axis runs over, the one named last changes fastest.
Arguments:
- features: bfloat16 [256, 256, 1024], P('lat', 'lon'), may hold values from -28 to 28
- w_qkv: bfloat16 [1024, 3072], replicated, may hold values from -0.078125 to 0.078125
- cotangent: bfloat16 [256, 256, 1024], P('lat', 'lon'), may hold values from -6 to 6
- row_reach: int32 [256], replicated, may hold values from 1 to 4, as said below
- col_reach: int32 [256], replicated, may hold values from 1 to 8, as said below
Outputs:
- attended: bfloat16 [256, 256, 1024], P('lat', 'lon')
- feature_grad: bfloat16 [256, 256, 1024], P('lat', 'lon')
Inputs may be any that keep to these rules, and one draw needn't show every extreme that they name: `row_reach`: equal to 4 in the first and last rows. `col_reach`: equal to 8 in the first and last rows.
All inputs are finite; a program needn't handle non-finite values.
Results may differ from a plain program's by a relative error of at most 0.012.
The roundings to bfloat16 on the way count: a program that leaves them out, or rounds other values in their place, can miss the bound.
Values may be sent and summed in bfloat16 or wider, within the bound.
A program may use at most 128 MiB of HBM per device.

v0:
```python
import math

import jax
import jax.numpy as jnp
from jax import lax
from jax.sharding import PartitionSpec as P

HEADS = 16
RMAX = 4
CMAX = 8


def extended(block, sides, width, periodic):
    for axis, dim in sides:
        count = lax.axis_size(axis)
        forward = [(i, i + 1) for i in range(count - 1)]
        if periodic:
            forward.append((count - 1, 0))
        backward = [(target, source) for source, target in forward]
        low = lax.ppermute(
            lax.slice_in_dim(block, block.shape[dim] - width, None, axis=dim), axis, forward
        )
        high = lax.ppermute(lax.slice_in_dim(block, 0, width, axis=dim), axis, backward)
        block = jnp.concatenate([low, block, high], axis=dim)
    return block


def widen_block(local_block):
    lat_wide = extended(local_block, (("lat", 0),), RMAX, False)
    return extended(lat_wide, (("lon", 1),), CMAX, True)


def return_cols(kv_grads):
    n_wide = kv_grads.shape[1] - 2 * CMAX
    rim_cells = jnp.concatenate([kv_grads[:, :CMAX], kv_grads[:, n_wide + CMAX :]], 1)
    arrived = extended(rim_cells.astype(jnp.bfloat16), (("lon", 1),), CMAX, True).astype(
        rim_cells.dtype
    )
    inner_part = kv_grads[:, CMAX : CMAX + n_wide]
    inner_part = inner_part.at[:, :CMAX].add(arrived[:, :CMAX])
    return inner_part.at[:, n_wide - CMAX :].add(arrived[:, 3 * CMAX :])


def return_rows(kv_grads):
    n_tall = kv_grads.shape[0] - 2 * RMAX
    rim_cells = jnp.concatenate([kv_grads[:RMAX], kv_grads[n_tall + RMAX :]], 0)
    arrived = extended(rim_cells.astype(jnp.bfloat16), (("lat", 0),), RMAX, False).astype(
        rim_cells.dtype
    )
    inner_part = kv_grads[RMAX : RMAX + n_tall]
    inner_part = inner_part.at[:RMAX].add(arrived[:RMAX])
    return inner_part.at[n_tall - RMAX :].add(arrived[3 * RMAX :])


def shards(features, w_qkv, cotangent, row_reach, col_reach):
    n_rows, n_cols, n_chan = features.shape
    height = n_rows * lax.axis_size("lat")
    head_dim = n_chan // HEADS
    score_scale = 1.0 / math.sqrt(head_dim)
    first_row = lax.axis_index("lat") * n_rows
    flat_feat = features.reshape(-1, n_chan)
    qkv_rows = jnp.dot(flat_feat, w_qkv, preferred_element_type=jnp.float32).astype(jnp.bfloat16)
    queries = qkv_rows[:, :n_chan]
    wide_grid = widen_block(qkv_rows[:, n_chan:].reshape(n_rows, n_cols, 2 * n_chan))
    e_rows, e_cols = (wide_grid.shape[0], wide_grid.shape[1])
    wide_kv = wide_grid.reshape(-1, 2 * n_chan)
    q_cells = queries.reshape(-1, HEADS, head_dim)
    g_cells = cotangent.reshape(-1, HEADS, head_dim)
    key_cells = wide_kv[:, :n_chan].reshape(-1, HEADS, head_dim)
    val_cells = wide_kv[:, n_chan:].reshape(-1, HEADS, head_dim)
    reach_r = lax.dynamic_slice_in_dim(row_reach, first_row, n_rows)
    reach_c = lax.dynamic_slice_in_dim(col_reach, first_row, n_rows)
    local_rows = jnp.arange(n_rows, dtype=jnp.int32)
    wide_rows = jnp.arange(e_rows, dtype=jnp.int32)
    row_gap = wide_rows[None, :] - RMAX - local_rows[:, None]
    key_global = first_row + wide_rows - RMAX
    row_ok = (jnp.abs(row_gap) <= reach_r[:, None]) & ((key_global >= 0) & (key_global < height))[
        None, :
    ]
    col_gap = (
        jnp.arange(e_cols, dtype=jnp.int32)[None, :]
        - CMAX
        - jnp.arange(n_cols, dtype=jnp.int32)[:, None]
    )
    col_ok = jnp.abs(col_gap)[None] <= reach_c[:, None, None]
    usable = row_ok[:, None, :, None] & col_ok[:, :, None, :]
    usable = usable.reshape(n_rows * n_cols, e_rows * e_cols)
    scores = (
        jnp.einsum("qhe,khe->hqk", q_cells, key_cells, preferred_element_type=jnp.float32)
        * score_scale
    )
    scores = jnp.where(usable[None], scores, -1e30)
    row_peak = jnp.max(scores, axis=-1, keepdims=True)
    expo_terms = jnp.exp(scores - row_peak)
    probs = expo_terms / jnp.sum(expo_terms, axis=-1, keepdims=True)
    probs_b = probs.astype(jnp.bfloat16)
    attended = jnp.einsum("hqk,khe->qhe", probs_b, val_cells, preferred_element_type=jnp.float32)
    attended = attended.astype(jnp.bfloat16).reshape(n_rows, n_cols, n_chan)
    d_prob = jnp.einsum("qhe,khe->hqk", g_cells, val_cells, preferred_element_type=jnp.float32)
    delta_sum = jnp.sum(probs * d_prob, axis=-1, keepdims=True)
    d_score = (probs * (d_prob - delta_sum) * score_scale).astype(jnp.bfloat16)
    d_query = jnp.einsum("hqk,khe->qhe", d_score, key_cells, preferred_element_type=jnp.float32)
    d_key = jnp.einsum("hqk,qhe->khe", d_score, q_cells, preferred_element_type=jnp.float32)
    d_value = jnp.einsum("hqk,qhe->khe", probs_b, g_cells, preferred_element_type=jnp.float32)
    kv_grads = jnp.concatenate(
        [d_key.reshape(e_rows, e_cols, n_chan), d_value.reshape(e_rows, e_cols, n_chan)], -1
    )
    own_grads = return_rows(return_cols(kv_grads))
    d_qkv = jnp.concatenate([d_query.reshape(n_rows, n_cols, n_chan), own_grads], -1)
    d_qkv = d_qkv.astype(jnp.bfloat16).reshape(-1, 3 * n_chan)
    feature_grad = lax.dot_general(
        d_qkv, w_qkv, (((1,), (1,)), ((), ())), preferred_element_type=jnp.float32
    )
    feature_grad = feature_grad.astype(jnp.bfloat16).reshape(n_rows, n_cols, n_chan)
    return (attended, feature_grad)


def solution(mesh):
    placed = (P("lat", "lon", None), P(), P("lat", "lon", None), P(), P())
    return jax.shard_map(
        shards,
        mesh=mesh,
        in_specs=placed,
        out_specs=(P("lat", "lon", None), P("lat", "lon", None)),
        check_vma=False,
    )
```

profile of v0, /device:TPU:8, one launch (start us, length us, event | category | flops | bytes accessed | tf_op | source)
XLA Modules:
  0.0 219.7 jit_solution(378168042940530310)
XLA Ops:
  1.7 4.6 %convolution_convert_fusion = bf16[256,3072]{1,0:T(8,128)(2,1)S(1)} fusion(bf16[256,1024]{1,0:T(8,128)(2,1)S(1)} %bitcast.64, bf16[1024,3072]{1,0:T(8,128)(2,1)} %param.14), kind=kOutput, calls=%fused_computation.17 | convolution fusion | flops 1611399168 | bytes 8388608 | tf_op jit(solution)/shard_map/dot_general | solution.py:62
  7.0 4.0 %collective-permute-start.1 = (bf16[4,16,2048]{2,1,0:T(8,128)(2,1)}, bf16[4,16,2048]{2,1,0:T(8,128)(2,1)S(1)}, u32[]{:S(2)}, u32[]{:S(2)}) collective-permute-start(bf16[4,16,2048]{2,1,0:T(8,128)(2,1)} %bitcast.3), channel_id=1, source_target_pairs={{16,0},{32,16},{48,32},{64,48},{80,64},{96,80},{112,96},{128,112},... | collective-permute-start | bytes 786440 | tf_op jit(solution)/shard_map/ppermute | solution.py:23
  11.0 1.9 collective-permute-start
  15.2 5.6 %collective-permute-done = bf16[4,16,2048]{2,1,0:T(8,128)(2,1)S(1)} collective-permute-done((bf16[4,16,2048]{2,1,0:T(8,128)(2,1)S(1)}, bf16[4,16,2048]{2,1,0:T(8,128)(2,1)S(1)}, u32[]{:S(2)}, u32[]{:S(2)}) %collective-permute-start) | collective-permute-done | bytes 262176 | tf_op jit(solution)/shard_map/ppermute | solution.py:20
  24.2 8.2 %collective-permute-start.3 = (bf16[24,8,2048]{2,1,0:T(8,128)(2,1)}, bf16[24,8,2048]{2,1,0:T(8,128)(2,1)}, u32[]{:S(2)}, u32[]{:S(2)}) collective-permute-start(bf16[24,8,2048]{2,1,0:T(8,128)(2,1)} %get-tuple-element.59), channel_id=1, source_target_pairs={{1,0},{2,1},{3,2},{4,3},{5,4},{6,5},{7,6},{8,7},{9,8},{10,9},{11,1... | collective-permute-start | bytes 2359304 | tf_op jit(solution)/shard_map/ppermute | solution.py:23
  34.0 1.9 reshape.274
  38.6 4.2 %collective-permute-done.2 = bf16[24,8,2048]{2,1,0:T(8,128)(2,1)} collective-permute-done((bf16[24,8,2048]{2,1,0:T(8,128)(2,1)}, bf16[24,8,2048]{2,1,0:T(8,128)(2,1)}, u32[]{:S(2)}, u32[]{:S(2)}) %collective-permute-start.2) | collective-permute-done | bytes 786464 | tf_op jit(solution)/shard_map/ppermute | solution.py:20
  47.8 10.2 %fusion.53 = (f32[16,256]{1,0:T(8,128)S(1)}, f32[16,256,768]{2,1,0:T(8,128)}) fusion(pred[256,768]{1,0:T(8,128)(4,1)S(1)} %and.58, bf16[256,16,64]{0,2,1:T(8,128)(2,1)} %bitcast.73, bf16[768,16,64]{0,2,1:T(8,128)(2,1)S(1)} %bitcast.71), kind=kOutput, calls=%fused_computation.71 | convolution fusion | flops 415236864 | bytes 14893056 | tf_op jit(solution)/shard_map/sub | solution.py:94
  58.0 6.4 %fusion.17 = f32[768,16,64]{0,2,1:T(8,128)S(1)} fusion(bf16[256,16,64]{0,2,1:T(8,128)(2,1)} %copy.19, f32[16,256,768]{2,1,0:T(8,128)} %get-tuple-element.63, f32[16,256]{1,0:T(8,128)S(1)} %get-tuple-element.62), kind=kOutput, calls=%fused_computation.24 | convolution fusion | flops 408944640 | bytes 16269312 | tf_op jit(solution)/shard_map/hqk,qhe->khe/dot_general | solution.py:104
  64.4 5.1 %copy.23 = f32[768,16,64]{2,1,0:T(8,128)} copy(f32[768,16,64]{0,2,1:T(8,128)S(1)} %fusion.17) | data formatting | bytes 6291456 | tf_op jit(solution)/shard_map/hqk,qhe->khe/transpose | solution.py:104
  69.5 4.8 %reshape.276 = f32[24,32,1024]{2,1,0:T(8,128)S(1)} reshape(f32[768,16,64]{2,1,0:T(8,128)} %copy.23) | data formatting | bytes 6291456 | tf_op jit(solution)/shard_map/reshape | solution.py:106
  74.3 7.9 %fusion.54 = f32[16,768,256]{1,2,0:T(8,128)} fusion(bf16[768,16,64]{0,2,1:T(8,128)(2,1)} %bitcast.68, bf16[256,16,64]{0,2,1:T(8,128)(2,1)} %copy.19), kind=kOutput, calls=%fused_computation.72 | convolution fusion | flops 402653184 | bytes 14680064 | tf_op jit(solution)/shard_map/qhe,khe->hqk/dot_general | solution.py:99
  82.3 40.2 %fusion.16 = f32[768,16,64]{0,2,1:T(8,128)} fusion(bf16[256,16,64]{0,2,1:T(8,128)(2,1)} %bitcast.74, f32[16,768,256]{1,2,0:T(8,128)} %fusion.54, f32[16,256,768]{2,1,0:T(8,128)} %get-tuple-element.63, f32[16,256]{1,0:T(8,128)S(1)} %get-tuple-element.62), kind=kOutput, calls=%fused_computation.23 | convolution fusion | flops 424678144 | bytes 28852224 | tf_op jit(solution)/shard_map/hqk,qhe->khe/dot_general | solution.py:103
  122.5 6.8 %copy.21 = f32[768,16,64]{2,1,0:T(8,128)} copy(f32[768,16,64]{0,2,1:T(8,128)} %fusion.16) | data formatting | bytes 6291456 | tf_op jit(solution)/shard_map/hqk,qhe->khe/transpose | solution.py:103
  129.3 6.3 %reshape.275 = f32[24,32,1024]{2,1,0:T(8,128)} reshape(f32[768,16,64]{2,1,0:T(8,128)} %copy.21) | data formatting | bytes 6291456 | tf_op jit(solution)/shard_map/reshape | solution.py:106
  135.6 2.4 %constant_dynamic-update-slice_fusion.1 = f32[24,32,2048]{2,1,0:T(8,128)S(1)} fusion(f32[24,32,1024]{2,1,0:T(8,128)} %reshape.275), kind=kLoop, calls=%fused_computation.55 | loop fusion | bytes 6291456
  140.0 5.6 %collective-permute-start.5 = (bf16[24,8,2048]{2,1,0:T(8,128)(2,1)}, bf16[24,8,2048]{2,1,0:T(8,128)(2,1)}, u32[]{:S(2)}, u32[]{:S(2)}) collective-permute-start(bf16[24,8,2048]{2,1,0:T(8,128)(2,1)} %get-tuple-element.53), channel_id=1, source_target_pairs={{1,0},{2,1},{3,2},{4,3},{5,4},{6,5},{7,6},{8,7},{9,8},{10,9},{11,1... | collective-permute-start | bytes 2359304 | tf_op jit(solution)/shard_map/ppermute | solution.py:23
  145.6 3.1 %fusion.35 = bf16[256,16,64]{0,2,1:T(8,128)(2,1)} fusion(bf16[768,16,64]{0,2,1:T(8,128)(2,1)S(1)} %bitcast.69, f32[16,256,768]{2,1,0:T(8,128)S(1)} %bitcast.79, f32[16,256]{1,0:T(8,128)S(1)} %get-tuple-element.62), kind=kOutput, calls=%fused_computation.39 | convolution fusion | flops 409206784 | bytes 14696448 | tf_op jit(solution)/shard_map/hqk,khe->qhe/dot_general | solution.py:97
  148.9 2.9 %copy.18 = bf16[256,16,64]{2,1,0:T(8,128)(2,1)} copy(bf16[256,16,64]{0,2,1:T(8,128)(2,1)} %fusion.35) | data formatting | bytes 1048576 | tf_op jit(solution)/shard_map/convert_element_type | solution.py:98
  151.8 2.6 %reshape.273 = bf16[16,16,1024]{2,1,0:T(8,128)(2,1)} reshape(bf16[256,16,64]{2,1,0:T(8,128)(2,1)} %copy.18) | data formatting | bytes 1048576 | tf_op jit(solution)/shard_map/reshape | solution.py:98
  162.1 14.2 %collective-permute-start.7 = (bf16[4,16,2048]{2,1,0:T(8,128)(2,1)}, bf16[4,16,2048]{2,1,0:T(8,128)(2,1)}, u32[]{:S(2)}, u32[]{:S(2)}) collective-permute-start(bf16[4,16,2048]{2,1,0:T(8,128)(2,1)} %get-tuple-element.57), channel_id=1, source_target_pairs={{16,0},{32,16},{48,32},{64,48},{80,64},{96,80},{112,96},{128,112},... | collective-permute-start | bytes 786440 | tf_op jit(solution)/shard_map/ppermute | solution.py:23
  176.3 33.4 %fusion.32 = bf16[16,64,256]{2,1,0:T(8,128)(2,1)} fusion(bf16[768,16,64]{0,2,1:T(8,128)(2,1)} %bitcast.70, f32[16,768,256]{1,2,0:T(8,128)} %fusion.54, f32[16,256,768]{2,1,0:T(8,128)} %get-tuple-element.63, f32[16,256]{1,0:T(8,128)S(1)} %get-tuple-element.62), kind=kOutput, calls=%fused_computation.37 | convolution fusion | flops 424940288 | bytes 27279360 | tf_op jit(solution)/shard_map/hqk,khe->qhe/dot_general | solution.py:102
  209.7 2.0 copy.24
  214.3 5.5 %fusion.26 = bf16[256,1024]{1,0:T(8,128)(2,1)} fusion(bf16[1024,3072]{1,0:T(8,128)(2,1)} %param.14, bf16[256,2048]{1,0:T(8,128)(2,1)S(1)} %bitcast.72, bf16[256,1024]{1,0:T(8,128)(2,1)S(1)} %copy-done.6), kind=kOutput, calls=%fused_computation.35 | convolution fusion | flops 1614020608 | bytes 8388608 | tf_op jit(solution)/shard_map/dot_general | solution.py:111
  (68 shorter events, 28.9 us)
Async XLA Ops:
  0.6 1.1 copy-start
  6.3 14.8 %copy-start.4 = (bf16[256,3072]{1,0:T(8,128)(2,1)}, bf16[256,3072]{1,0:T(8,128)(2,1)S(1)}, u32[]{:S(2)}) copy-start(bf16[256,3072]{1,0:T(8,128)(2,1)S(1)} %convolution_convert_fusion) | copy-start | bytes 4718596
  6.3 6.8 %copy-start.7 = (s32[256]{0:T(256)S(1)}, s32[256]{0:T(256)}, u32[]{:S(2)}) copy-start(s32[256]{0:T(256)} %param.16) | copy-start | bytes 3076
  6.3 6.9 %copy-start.8 = (s32[256]{0:T(256)S(1)}, s32[256]{0:T(256)}, u32[]{:S(2)}) copy-start(s32[256]{0:T(256)} %param.17) | copy-start | bytes 3076
  7.0 8.2 %collective-permute-start.1 = (bf16[4,16,2048]{2,1,0:T(8,128)(2,1)}, bf16[4,16,2048]{2,1,0:T(8,128)(2,1)S(1)}, u32[]{:S(2)}, u32[]{:S(2)}) collective-permute-start(bf16[4,16,2048]{2,1,0:T(8,128)(2,1)} %bitcast.3), channel_id=1, source_target_pairs={{16,0},{32,16},{48,32},{64,48},{80,64},{96,80},{112,96},{128,112},... | collective-permute-start | bytes 786440 | tf_op jit(solution)/shard_map/ppermute | solution.py:23
  11.0 9.8 %collective-permute-start = (bf16[4,16,2048]{2,1,0:T(8,128)(2,1)S(1)}, bf16[4,16,2048]{2,1,0:T(8,128)(2,1)S(1)}, u32[]{:S(2)}, u32[]{:S(2)}) collective-permute-start(bf16[4,16,2048]{2,1,0:T(8,128)(2,1)S(1)} %bitcast.76), channel_id=1, source_target_pairs={{0,16},{16,32},{32,48},{48,64},{64,80},{80,96},{96,112},{112,128},... | collective-permute-start | bytes 786440 | tf_op jit(solution)/shard_map/ppermute | solution.py:20
  22.3 15.3 %slice-start = ((bf16[256,3072]{1,0:T(8,128)(2,1)}), bf16[256,1024]{1,0:T(8,128)(2,1)S(1)}, s32[]{:S(2)}) async-start(bf16[256,3072]{1,0:T(8,128)(2,1)} %copy-done.4), calls=%async_computation | async-start | bytes 1048576 | tf_op jit(solution)/shard_map/slice | solution.py:63
  22.3 20.6 %collective-permute-start.2 = (bf16[24,8,2048]{2,1,0:T(8,128)(2,1)}, bf16[24,8,2048]{2,1,0:T(8,128)(2,1)}, u32[]{:S(2)}, u32[]{:S(2)}) collective-permute-start(bf16[24,8,2048]{2,1,0:T(8,128)(2,1)} %get-tuple-element.58), channel_id=1, source_target_pairs={{0,1},{1,2},{2,3},{3,4},{4,5},{5,6},{6,7},{7,8},{8,9},{9,10},{10,1... | collective-permute-start | bytes 2359304 | tf_op jit(solution)/shard_map/ppermute | solution.py:20
  24.2 18.6 %collective-permute-start.3 = (bf16[24,8,2048]{2,1,0:T(8,128)(2,1)}, bf16[24,8,2048]{2,1,0:T(8,128)(2,1)}, u32[]{:S(2)}, u32[]{:S(2)}) collective-permute-start(bf16[24,8,2048]{2,1,0:T(8,128)(2,1)} %get-tuple-element.59), channel_id=1, source_target_pairs={{1,0},{2,1},{3,2},{4,3},{5,4},{6,5},{7,6},{8,7},{9,8},{10,9},{11,1... | collective-permute-start | bytes 2359304 | tf_op jit(solution)/shard_map/ppermute | solution.py:23
  46.3 1.6 copy-start.5
  135.6 10.0 %slice-start.1 = ((s8[12582912]{0:T(1024)(128)(4,1)}), s8[4194304]{0:T(1024)(128)(4,1)S(1)}, s32[]{:S(2)}) async-start(s8[12582912]{0:T(1024)(128)(4,1)} %bitcast.78), calls=%async_computation.1 | async-start | bytes 8388608
  138.0 7.6 %slice-start.2 = ((s8[12582912]{0:T(1024)(128)(4,1)}), s8[4194304]{0:T(1024)(128)(4,1)S(1)}, s32[]{:S(2)}) async-start(s8[12582912]{0:T(1024)(128)(4,1)} %bitcast.78), calls=%async_computation.2 | async-start | bytes 8388608
  138.2 10.5 %copy-start.2 = (f32[24,32,2048]{2,1,0:T(8,128)}, f32[24,32,2048]{2,1,0:T(8,128)S(1)}, u32[]{:S(2)}) copy-start(f32[24,32,2048]{2,1,0:T(8,128)S(1)} %constant_dynamic-update-slice_fusion) | copy-start | bytes 18874372
  138.2 7.4 %slice-start.3 = ((s8[12582912]{0:T(1024)(128)(4,1)}), s8[4194304]{0:T(1024)(128)(4,1)S(1)}, s32[]{:S(2)}) async-start(s8[12582912]{0:T(1024)(128)(4,1)} %bitcast.78), calls=%async_computation.3 | async-start | bytes 8388608
  138.7 6.9 %copy-start.3 = (bf16[768,1024]{0,1:T(8,128)(2,1)S(1)}, bf16[768,1024]{0,1:T(8,128)(2,1)}, u32[]{:S(2)}) copy-start(bf16[768,1024]{0,1:T(8,128)(2,1)} %copy.26) | copy-start | bytes 4718596
  140.0 15.9 %collective-permute-start.4 = (bf16[24,8,2048]{2,1,0:T(8,128)(2,1)}, bf16[24,8,2048]{2,1,0:T(8,128)(2,1)}, u32[]{:S(2)}, u32[]{:S(2)}) collective-permute-start(bf16[24,8,2048]{2,1,0:T(8,128)(2,1)} %get-tuple-element.52), channel_id=1, source_target_pairs={{0,1},{1,2},{2,3},{3,4},{4,5},{5,6},{6,7},{7,8},{8,9},{9,10},{10,1... | collective-permute-start | bytes 2359304 | tf_op jit(solution)/shard_map/ppermute | solution.py:20
  140.0 15.9 %collective-permute-start.5 = (bf16[24,8,2048]{2,1,0:T(8,128)(2,1)}, bf16[24,8,2048]{2,1,0:T(8,128)(2,1)}, u32[]{:S(2)}, u32[]{:S(2)}) collective-permute-start(bf16[24,8,2048]{2,1,0:T(8,128)(2,1)} %get-tuple-element.53), channel_id=1, source_target_pairs={{1,0},{2,1},{3,2},{4,3},{5,4},{6,5},{7,6},{8,7},{9,8},{10,9},{11,1... | collective-permute-start | bytes 2359304 | tf_op jit(solution)/shard_map/ppermute | solution.py:23
  160.2 51.8 %collective-permute-start.6 = (bf16[4,16,2048]{2,1,0:T(8,128)(2,1)S(1)}, bf16[4,16,2048]{2,1,0:T(8,128)(2,1)}, u32[]{:S(2)}, u32[]{:S(2)}) collective-permute-start(bf16[4,16,2048]{2,1,0:T(8,128)(2,1)S(1)} %get-tuple-element.56), channel_id=1, source_target_pairs={{0,16},{16,32},{32,48},{48,64},{64,80},{80,96},{96,112},{112,128},... | collective-permute-start | bytes 786440 | tf_op jit(solution)/shard_map/ppermute | solution.py:20
  162.1 49.9 %collective-permute-start.7 = (bf16[4,16,2048]{2,1,0:T(8,128)(2,1)}, bf16[4,16,2048]{2,1,0:T(8,128)(2,1)}, u32[]{:S(2)}, u32[]{:S(2)}) collective-permute-start(bf16[4,16,2048]{2,1,0:T(8,128)(2,1)} %get-tuple-element.57), channel_id=1, source_target_pairs={{16,0},{32,16},{48,32},{64,48},{80,64},{96,80},{112,96},{128,112},... | collective-permute-start | bytes 786440 | tf_op jit(solution)/shard_map/ppermute | solution.py:23
  213.0 1.3 copy-start.6
  214.3 5.5 %copy-start.1 = (bf16[16,16,1024]{2,1,0:T(8,128)(2,1)S(1)}, bf16[16,16,1024]{2,1,0:T(8,128)(2,1)}, u32[]{:S(2)}) copy-start(bf16[16,16,1024]{2,1,0:T(8,128)(2,1)} %param.13) | copy-start | bytes 1572868
where the time goes:
time: 221 us; the launch traced here: 220 us
  matrix products  111 us (50%)
  local copies, waits for them, and re-layouts  48 us (22%)
  starting transfers between devices  37.8 us (17%)
  waiting for transfers between devices  13.2 us (6%)
  other arithmetic  8.61 us (4%)
    dot_general x1, matrix products, shards(): jnp.einsum('hqk,qhe->khe', d_score, q_cells, preferred_element_type=jnp.f...  40.2 us
    dot_general x1, matrix products, shards(): jnp.einsum('hqk,khe->qhe', d_score, key_cells, preferred_element_type=jnp...  33.4 us
    ppermute x4, starting transfers between devices, extended(): lax.ppermute(lax.slice_in_dim(block, 0, width, axis=dim), axis, backward)  32 us
    ppermute x4, waiting for transfers between devices, extended(): lax.ppermute(lax.slice_in_dim(block, block.shape[dim] - width, None, axis...  11.3 us
    sub x1, matrix products, shards(): expo_terms = jnp.exp(scores - row_peak)  10.2 us
    dot_general x1, matrix products, shards(): jnp.einsum('qhe,khe->hqk', g_cells, val_cells, preferred_element_type=jnp...  7.95 us
    transpose x1, local copies, waits for them, and re-layouts, shards(): jnp.einsum('hqk,qhe->khe', d_score, q_cells, preferred_element_type=jnp.f...  6.81 us
    unnamed x27, local copies, waits for them, and re-layouts  6.66 us
  transfers between devices with their start and end apart: 8, of which 4 were waited for; matrix products, arithmetic and copies ran while one was open for 23% of the time, Pallas kernels for 0%

commit v1 on v0

v1 whole, which is shorter than its diff:
```python
import jax
import jax.numpy as jnp
from jax import lax
from jax.experimental import pallas as pl
from jax.experimental.pallas import tpu as pltpu
from jax.sharding import PartitionSpec as P

HEADS = 16
RMAX = 4
CMAX = 8
CHAN = 1024
GROUP = 256
NGROUP = CHAN // GROUP
F32 = jnp.float32
BF16 = jnp.bfloat16
MESH = pl.DeviceIdType.MESH
NN = (((1,), (0,)), ((), ()))
NT = (((1,), (1,)), ((), ()))
TN = (((0,), (0,)), ((), ()))


def dot(a, b, dims):
    return lax.dot_general(a, b, dims, preferred_element_type=F32)


def block_diagonal(x):
    rows = lax.broadcasted_iota(jnp.int32, (256, GROUP), 0) // 64
    cols = lax.broadcasted_iota(jnp.int32, (256, GROUP), 1) // 64
    return jnp.where(rows == cols, jnp.concatenate([x] * 4, 0), jnp.zeros((), x.dtype))


def take_diagonal(o):
    cols = lax.broadcasted_iota(jnp.int32, (64, GROUP), 1) // 64
    out = o[:64]
    for head in range(1, 4):
        out = jnp.where(cols == head, o[64 * head : 64 * head + 64], out)
    return out


def kernel(
    x_hbm, w_hbm, g_ref, rr_ref, cc_ref, att_ref, fg_ref,
    xm, xl, xr, edge_l, edge_r, w, q, k, v, dk, dv, dq, bias, grads,
    tb_send, tb_recv, side_send, side_recv,
    local_sem, send_sem, recv_sem,
):
    lat, lon = lax.axis_index("lat"), lax.axis_index("lon")
    n_lat, n_lon = lax.axis_size("lat"), lax.axis_size("lon")
    up = (lax.rem(lat + n_lat - 1, n_lat), lon)
    down = (lax.rem(lat + 1, n_lat), lon)
    left = (lat, lax.rem(lon + n_lon - 1, n_lon))
    right = (lat, lax.rem(lon + 1, n_lon))

    own_copy = pltpu.make_async_copy(x_hbm, xm.at[4:20], local_sem.at[0])
    own_copy.start()
    w_copies = []
    for part in range(3):
        cols = slice(part * CHAN, (part + 1) * CHAN)
        w_copies.append(
            pltpu.make_async_copy(w_hbm.at[:, cols], w.at[:, cols], local_sem.at[1 + part])
        )
        w_copies[-1].start()

    barrier = pltpu.get_barrier_semaphore()
    for device in (up, down, left, right):
        pl.semaphore_signal(barrier, inc=1, device_id=device, device_id_type=MESH)
    own_copy.wait()
    for row in range(16):
        edge_l[8 * row : 8 * row + 8] = xm[4 + row, 0:8]
        edge_r[8 * row : 8 * row + 8] = xm[4 + row, 8:16]
    pl.semaphore_wait(barrier, 4)

    def send(index, src, dst, device):
        copy = pltpu.make_async_remote_copy(
            src_ref=src,
            dst_ref=dst,
            send_sem=send_sem.at[index],
            recv_sem=recv_sem.at[index],
            device_id=device,
            device_id_type=MESH,
        )
        copy.start()
        return copy

    to_left = send(0, edge_l, xr.at[32:160], left)
    to_right = send(1, edge_r, xl.at[32:160], right)
    to_up = send(2, xm.at[4:8], xm.at[20:24], up)
    to_down = send(3, xm.at[16:20], xm.at[0:4], down)

    dk[...] = jnp.zeros_like(dk)
    dv[...] = jnp.zeros_like(dv)

    first_row = lat * 16
    height = n_lat * 16
    lane = lax.broadcasted_iota(jnp.int32, (1, 128), 1)
    q_row, q_col = lane % 64 // 16, lane % 16
    cell = lax.broadcasted_iota(jnp.int32, (384, 1), 0)
    k_row, k_pos = cell // 32, cell % 32
    k_col = jnp.where(k_pos < 16, k_pos, jnp.where(k_pos < 24, k_pos - 24, k_pos - 8))
    row_gap = jnp.abs(k_row - RMAX - q_row)
    col_gap = jnp.abs(k_col - q_col)
    for b in range(4):
        reach_r = jnp.zeros((1, 128), jnp.int32)
        reach_c = jnp.zeros((1, 128), jnp.int32)
        for row in range(4):
            reach_r = jnp.where(q_row == row, rr_ref[first_row + 4 * b + row], reach_r)
            reach_c = jnp.where(q_row == row, cc_ref[first_row + 4 * b + row], reach_c)
        key_row = first_row + 4 * b - RMAX + k_row
        ok = (row_gap <= reach_r) & (col_gap <= reach_c) & ((key_row >= 0) & (key_row < height))
        bias[b] = jnp.where(ok, 0.0, -1e30)

    for copy in w_copies:
        copy.wait()

    def w_cols(part, i):
        return w[:, pl.ds(pl.multiple_of(part * CHAN + i * GROUP, GROUP), GROUP)]

    def project_own(i, _):
        own = xm[4:20].reshape(256, CHAN)
        q[i] = dot(own, w_cols(0, i), NN).astype(BF16) * BF16(0.125)
        k[i, 4:20, 0:16] = dot(own, w_cols(1, i), NN).astype(BF16).reshape(16, 16, GROUP)
        v[i, 4:20, 0:16] = dot(own, w_cols(2, i), NN).astype(BF16).reshape(16, 16, GROUP)
        return 0

    lax.fori_loop(0, NGROUP, project_own, 0)

    to_left.wait_recv()
    to_right.wait_recv()
    corners = [
        send(4, xl.at[32:64], xl.at[160:192], up),
        send(5, xr.at[32:64], xr.at[160:192], up),
        send(6, xl.at[128:160], xl.at[0:32], down),
        send(7, xr.at[128:160], xr.at[0:32], down),
    ]

    def project_sides(i, _):
        for part, out in ((1, k), (2, v)):
            wt = w_cols(part, i)
            sides = jnp.concatenate([xl[32:160], xr[32:160]], 0)
            r = dot(sides, wt, NN).reshape(32, 8, GROUP).astype(BF16)
            out[i, 4:20, 16:24] = r[:16]
            out[i, 4:20, 24:32] = r[16:]
        return 0

    lax.fori_loop(0, NGROUP, project_sides, 0)

    to_up.wait_recv()
    to_down.wait_recv()
    for copy in corners:
        copy.wait_recv()

    def project_caps(i, _):
        for part, out in ((1, k), (2, v)):
            wt = w_cols(part, i)
            cells = jnp.concatenate(
                [xm[0:4].reshape(64, CHAN), xm[20:24].reshape(64, CHAN), xl[0:32], xl[160:192], xr[0:32], xr[160:192]], 0
            )
            r = dot(cells, wt, NN)
            mid = r[:128].astype(BF16).reshape(8, 16, GROUP)
            rim = r[128:].reshape(16, 8, GROUP).astype(BF16)
            out[i, 0:4, 0:16] = mid[:4]
            out[i, 20:24, 0:16] = mid[4:]
            out[i, 0:4, 16:24] = rim[0:4]
            out[i, 20:24, 16:24] = rim[4:8]
            out[i, 0:4, 24:32] = rim[8:12]
            out[i, 20:24, 24:32] = rim[12:16]
        return 0

    lax.fori_loop(0, NGROUP, project_caps, 0)

    def attend(b, hg):
        lanes = pl.ds(pl.multiple_of(hg * GROUP, GROUP), GROUP)
        window = slice(4 * b, 4 * b + 12)
        keys = k[hg, window].reshape(384, GROUP)
        vals = v[hg, window].reshape(384, GROUP)
        qd = block_diagonal(q[hg, 64 * b : 64 * b + 64])
        gd = block_diagonal(g_ref[4 * b : 4 * b + 4, :, lanes].reshape(64, GROUP))
        masked = bias[b]
        s = dot(keys, qd, NT) + jnp.concatenate([masked, masked], 1)
        e = jnp.exp(s - jnp.max(s, 0, keepdims=True))
        p = e * (1.0 / jnp.sum(e, 0, keepdims=True))
        dp = dot(vals, gd, NT)
        delta = jnp.sum(p * dp, 0, keepdims=True)
        ds = (p * (dp - delta)).astype(BF16)
        pb = p.astype(BF16)
        dk[hg, window] += dot(ds, qd, NN).reshape(12, 32, GROUP)
        dv[hg, window] += dot(pb, gd, NN).reshape(12, 32, GROUP)
        att_ref[64 * b : 64 * b + 64, lanes] = take_diagonal(dot(pb, vals, TN)).astype(BF16)
        dq[64 * b : 64 * b + 64, lanes] = (take_diagonal(dot(ds, keys, TN)) * 0.125).astype(BF16)

    def attend_block(b):
        def body(i, _):
            attend(b, 2 * i)
            attend(b, 2 * i + 1)
            return 0

        lax.fori_loop(0, NGROUP // 2, body, 0)

    attend_block(0)
    attend_block(3)

    for hg in range(NGROUP):
        for offset, src in ((CHAN, dk), (2 * CHAN, dv)):
            cols = slice(offset + hg * GROUP, offset + (hg + 1) * GROUP)
            grads[0:128, cols] = src[hg, 0:4].reshape(128, GROUP).astype(BF16)
            grads[128:256, cols] = src[hg, 20:24].reshape(128, GROUP).astype(BF16)

    def back_caps(n, _):
        lanes = pl.ds(pl.multiple_of(n * GROUP, GROUP), GROUP)
        r = dot(grads[:, CHAN:], w[lanes, CHAN:], NT).astype(BF16)
        tb_send[:, :, lanes] = r.reshape(8, 32, GROUP)
        return 0

    lax.fori_loop(0, NGROUP, back_caps, 0)
    back_up = send(8, tb_send.at[0:4], tb_recv.at[4:8], up)
    back_down = send(9, tb_send.at[4:8], tb_recv.at[0:4], down)

    attend_block(1)
    attend_block(2)

    for hg in range(NGROUP):
        for offset, src in ((CHAN, dk), (2 * CHAN, dv)):
            cols = slice(offset + hg * GROUP, offset + (hg + 1) * GROUP)
            grads[0:128, cols] = src[hg, 4:20, 16:24].reshape(128, GROUP).astype(BF16)
            grads[128:256, cols] = src[hg, 4:20, 24:32].reshape(128, GROUP).astype(BF16)
    back_up.wait_recv()
    back_down.wait_recv()

    def back_sides(n, _):
        lanes = pl.ds(pl.multiple_of(n * GROUP, GROUP), GROUP)
        r = dot(grads[:, CHAN:], w[lanes, CHAN:], NT)
        rim = tb_recv[:, 16:32, lanes].astype(F32)
        for side in range(2):
            half = r[128 * side : 128 * side + 128]
            part = rim[:, 8 * side : 8 * side + 8].reshape(64, GROUP)
            whole = jnp.concatenate([half[:32] + part[:32], half[32:96], half[96:] + part[32:]], 0)
            side_send[side, :, lanes] = whole.astype(BF16)
        return 0

    lax.fori_loop(0, NGROUP, back_sides, 0)
    back_left = send(10, side_send.at[0], side_recv.at[1], left)
    back_right = send(11, side_send.at[1], side_recv.at[0], right)

    grads[:, :CHAN] = dq[...]
    for hg in range(NGROUP):
        for offset, src in ((CHAN, dk), (2 * CHAN, dv)):
            cols = slice(offset + hg * GROUP, offset + (hg + 1) * GROUP)
            grads[:, cols] = src[hg, 4:20, 0:16].reshape(256, GROUP).astype(BF16)

    own_out = dk

    def back_own(n, _):
        lanes = pl.ds(pl.multiple_of(n * GROUP, GROUP), GROUP)
        r = dot(grads[...], w[lanes, :], NT)
        cap = tb_recv[:, 0:16, lanes].astype(F32).reshape(128, GROUP)
        whole = jnp.concatenate([r[:64] + cap[:64], r[64:192], r[192:] + cap[64:]], 0)
        own_out[n, 0:16, 0:16] = whole.reshape(16, 16, GROUP)
        return 0

    lax.fori_loop(0, NGROUP, back_own, 0)
    back_left.wait_recv()
    back_right.wait_recv()
    for n in range(NGROUP):
        lanes = slice(n * GROUP, (n + 1) * GROUP)
        for side in range(2):
            part = side_recv[side, :, lanes].astype(F32).reshape(16, 8, GROUP)
            own_out[n, 0:16, 8 * side : 8 * side + 8] += part
        fg_ref[:, lanes] = own_out[n, 0:16, 0:16].reshape(256, GROUP).astype(BF16)

    for copy in (to_left, to_right, to_up, to_down, *corners, back_up, back_down, back_left, back_right):
        copy.wait_send()


def shards(features, w_qkv, cotangent, row_reach, col_reach):
    vmem = pl.BlockSpec(memory_space=pltpu.VMEM)
    smem = pl.BlockSpec(memory_space=pltpu.SMEM)
    any_space = pl.BlockSpec(memory_space=pl.ANY)
    att, grad = pl.pallas_call(
        kernel,
        out_shape=[jax.ShapeDtypeStruct((256, CHAN), BF16)] * 2,
        in_specs=[any_space, any_space, vmem, smem, smem],
        out_specs=[vmem, vmem],
        scratch_shapes=[
            pltpu.VMEM((24, 16, CHAN), BF16),
            pltpu.VMEM((192, CHAN), BF16),
            pltpu.VMEM((192, CHAN), BF16),
            pltpu.VMEM((128, CHAN), BF16),
            pltpu.VMEM((128, CHAN), BF16),
            pltpu.VMEM((CHAN, 3 * CHAN), BF16),
            pltpu.VMEM((NGROUP, 256, GROUP), BF16),
            pltpu.VMEM((NGROUP, 24, 32, GROUP), BF16),
            pltpu.VMEM((NGROUP, 24, 32, GROUP), BF16),
            pltpu.VMEM((NGROUP, 24, 32, GROUP), F32),
            pltpu.VMEM((NGROUP, 24, 32, GROUP), F32),
            pltpu.VMEM((256, CHAN), BF16),
            pltpu.VMEM((4, 384, 128), F32),
            pltpu.VMEM((256, 3 * CHAN), BF16),
            pltpu.VMEM((8, 32, CHAN), BF16),
            pltpu.VMEM((8, 32, CHAN), BF16),
            pltpu.VMEM((2, 128, CHAN), BF16),
            pltpu.VMEM((2, 128, CHAN), BF16),
            pltpu.SemaphoreType.DMA((4,)),
            pltpu.SemaphoreType.DMA((12,)),
            pltpu.SemaphoreType.DMA((12,)),
        ],
        compiler_params=pltpu.CompilerParams(
            collective_id=0, has_side_effects=True, vmem_limit_bytes=56 << 20
        ),
        name="sphere_attention",
    )(features, w_qkv, cotangent, row_reach, col_reach)
    return att.reshape(features.shape), grad.reshape(features.shape)


def solution(mesh):
    placed = (P("lat", "lon", None), P(), P("lat", "lon", None), P(), P())
    return jax.shard_map(
        shards,
        mesh=mesh,
        in_specs=placed,
        out_specs=(P("lat", "lon", None), P("lat", "lon", None)),
        check_vma=False,
    )
```

time: 221 us -> 56.6 us (0.26)
  the two profiles are of different devices: /device:TPU:8 before, /device:TPU:1 now
where the time goes in v1:
time: 56.6 us; the launch traced here: 56.4 us
  Pallas kernels  52 us (92%)
  local copies, waits for them, and re-layouts  3.76 us (7%)
  between operations  0.64 us (1%)
    pallas_call x1, Pallas kernels, shards(): pl.pallas_call(kernel, out_shape=[jax.ShapeDtypeStruct((256, CHAN), BF16)...  52 us
    unnamed x2, local copies, waits for them, and re-layouts  3.76 us

profile of v1, /device:TPU:1, one launch (start us, length us, event | category | flops | bytes accessed | tf_op | source)
XLA Modules:
  0.0 56.4 jit_solution(16931809313177899198)
XLA Ops:
  0.6 52.0 %sphere_attention.1 = (bf16[256,1024]{1,0:T(8,128)(2,1)}, bf16[256,1024]{1,0:T(8,128)(2,1)}) custom-call(bf16[16,16,1024]{2,1,0:T(8,128)(2,1)} %x_hbm.1, bf16[1024,3072]{1,0:T(8,128)(2,1)} %w_hbm.1, bf16[16,16,1024]{2,1,0:T(8,128)(2,1)} %g_ref.1, s32[256]{0:T(256)} %rr_ref.1, s32[256]{0:T(256)} %cc_ref.1), custom_call_target="tpu_custom_call" | custom-call | tf_op jit(solution)/shard_map/sphere_attention/pallas_call | solution.py:277
  52.7 1.9 %copy.9 = bf16[16,16,1024]{2,1,0:T(8,128)(2,1)} copy(bf16[16,16,1024]{2,1,0:T(8,128)(2,1)} %bitcast.3) | data formatting | bytes 1048576
  54.5 1.9 %copy.10 = bf16[16,16,1024]{2,1,0:T(8,128)(2,1)} copy(bf16[16,16,1024]{2,1,0:T(8,128)(2,1)} %bitcast.2) | data formatting | bytes 1048576

commit v2 on v1

v2 whole, which is shorter than its diff:
```python
import jax
import jax.numpy as jnp
from jax import lax
from jax.experimental import pallas as pl
from jax.experimental.pallas import tpu as pltpu
from jax.sharding import PartitionSpec as P

HEADS = 16
RMAX = 4
CMAX = 8
CHAN = 1024
GROUP = 256
NGROUP = CHAN // GROUP
BLOCKS = 4
F32 = jnp.float32
BF16 = jnp.bfloat16
MESH = pl.DeviceIdType.MESH
NN = (((1,), (0,)), ((), ()))
NT = (((1,), (1,)), ((), ()))
TN = (((0,), (0,)), ((), ()))


def dot(a, b, dims):
    return lax.dot_general(a, b, dims, preferred_element_type=F32)


def block_diagonal(x):
    rows = lax.broadcasted_iota(jnp.int32, (256, GROUP), 0) // 64
    cols = lax.broadcasted_iota(jnp.int32, (256, GROUP), 1) // 64
    return jnp.where(rows == cols, jnp.concatenate([x] * 4, 0), jnp.zeros((), x.dtype))


def take_diagonal(o):
    cols = lax.broadcasted_iota(jnp.int32, (64, GROUP), 1) // 64
    out = o[:64]
    for head in range(1, 4):
        out = jnp.where(cols == head, o[64 * head : 64 * head + 64], out)
    return out


def kernel(
    x_hbm, w_hbm, g_hbm, rr_ref, cc_ref, att_ref, fg_ref,
    xm, xs, xc, edges, w, g, q, k, v, bias, probs, dscores,
    grads_cap, grads_side, grads_own, side_edge, own_out,
    cap_send, cap_recv, side_send, side_recv,
    local_sem, send_sem, recv_sem,
):
    lat, lon = lax.axis_index("lat"), lax.axis_index("lon")
    n_lat, n_lon = lax.axis_size("lat"), lax.axis_size("lon")
    up = (lax.rem(lat + n_lat - 1, n_lat), lon)
    down = (lax.rem(lat + 1, n_lat), lon)
    left = (lat, lax.rem(lon + n_lon - 1, n_lon))
    right = (lat, lax.rem(lon + 1, n_lon))

    barrier = pltpu.get_barrier_semaphore()
    for device in (up, down, left, right):
        pl.semaphore_signal(barrier, inc=1, device_id=device, device_id_type=MESH)

    def fetch(index, src, dst):
        copy = pltpu.make_async_copy(src, dst, local_sem.at[index])
        copy.start()
        return copy

    own_copy = fetch(0, x_hbm, xm)
    w_copies = []
    for part in range(3):
        cols = slice(part * CHAN, (part + 1) * CHAN)
        w_copies.append(fetch(1 + part, w_hbm.at[:, cols], w.at[:, cols]))
    g_copy = fetch(4, g_hbm, g)

    own_copy.wait()
    for row in range(16):
        edges[0, 8 * row : 8 * row + 8] = xm[16 * row : 16 * row + 8]
        edges[1, 8 * row : 8 * row + 8] = xm[16 * row + 8 : 16 * row + 16]
    pl.semaphore_wait(barrier, 4)

    sent = []

    def send(src, dst, device):
        index = len(sent)
        copy = pltpu.make_async_remote_copy(
            src_ref=src,
            dst_ref=dst,
            send_sem=send_sem.at[index],
            recv_sem=recv_sem.at[index],
            device_id=device,
            device_id_type=MESH,
        )
        copy.start()
        sent.append(copy)
        return copy

    to_left = send(edges.at[0], xs.at[128:256], left)
    to_right = send(edges.at[1], xs.at[0:128], right)
    to_up = send(xm.at[0:64], xc.at[64:128], up)
    to_down = send(xm.at[192:256], xc.at[0:64], down)

    first_row = lat * 16
    height = n_lat * 16
    lane = lax.broadcasted_iota(jnp.int32, (1, 128), 1)
    q_row, q_col = lane % 64 // 16, lane % 16
    cell = lax.broadcasted_iota(jnp.int32, (384, 1), 0)
    pair, place = cell // 64, cell % 64
    own = place < 32
    k_row = 2 * pair + jnp.where(own, place // 16, place % 16 // 8)
    k_col = jnp.where(own, place % 16, place % 8 + jnp.where(place < 48, -8, 16))
    row_gap = jnp.abs(k_row - RMAX - q_row)
    col_gap = jnp.abs(k_col - q_col)
    for b in range(BLOCKS):
        reach_r = jnp.zeros((1, 128), jnp.int32)
        reach_c = jnp.zeros((1, 128), jnp.int32)
        for row in range(4):
            reach_r = jnp.where(q_row == row, rr_ref[first_row + 4 * b + row], reach_r)
            reach_c = jnp.where(q_row == row, cc_ref[first_row + 4 * b + row], reach_c)
        key_row = first_row + 4 * b - RMAX + k_row
        ok = (row_gap <= reach_r) & (col_gap <= reach_c) & ((key_row >= 0) & (key_row < height))
        bias[b] = jnp.where(ok, 0.0, -1e30)

    def w_cols(part, i):
        return w[:, pl.ds(pl.multiple_of(part * CHAN + i * GROUP, GROUP), GROUP)]

    def project_query(i, _):
        r = dot(xm[...], w_cols(0, i), NN)
        q[i] = r.astype(BF16) * BF16(0.125)
        return 0

    def project_own(i, _):
        cells = xm[...]
        k[i, 2:10, 0:32] = dot(cells, w_cols(1, i), NN).astype(BF16).reshape(8, 32, GROUP)
        v[i, 2:10, 0:32] = dot(cells, w_cols(2, i), NN).astype(BF16).reshape(8, 32, GROUP)
        return 0

    w_copies[0].wait()
    lax.fori_loop(0, NGROUP, project_query, 0)
    w_copies[1].wait()
    w_copies[2].wait()
    lax.fori_loop(0, NGROUP, project_own, 0)

    to_left.wait_recv()
    to_right.wait_recv()
    corners = []
    for side in range(2):
        base = 128 * side
        corners.append(send(xs.at[base : base + 32], xc.at[160 + 64 * side : 192 + 64 * side], up))
        corners.append(send(xs.at[base + 96 : base + 128], xc.at[128 + 64 * side : 160 + 64 * side], down))

    def project_sides(i, _):
        for part, out in ((1, k), (2, v)):
            r = dot(xs[...], w_cols(part, i), NN).astype(BF16).reshape(16, 16, GROUP)
            out[i, 2:10, 32:48] = r[:8]
            out[i, 2:10, 48:64] = r[8:]
        return 0

    lax.fori_loop(0, NGROUP, project_sides, 0)
    g_copy.wait()

    def query_block(b, hg):
        return block_diagonal(q[hg, pl.ds(64 * b, 64)])

    def grad_block(b, hg):
        lanes = slice(hg * GROUP, (hg + 1) * GROUP) if isinstance(hg, int) else pl.ds(pl.multiple_of(hg * GROUP, GROUP), GROUP)
        return block_diagonal(g[pl.ds(4 * b, 4), :, lanes].reshape(64, GROUP))

    def attend(b, hg):
        keys = k[hg, pl.ds(2 * b, 6)].reshape(384, GROUP)
        vals = v[hg, pl.ds(2 * b, 6)].reshape(384, GROUP)
        masked = bias[b]
        s = dot(keys, query_block(b, hg), NT) + jnp.concatenate([masked, masked], 1)
        e = jnp.exp(s - jnp.max(s, 0, keepdims=True))
        p = e * (1.0 / jnp.sum(e, 0, keepdims=True))
        dp = dot(vals, grad_block(b, hg), NT)
        delta = jnp.sum(p * dp, 0, keepdims=True)
        dscores[b, hg] = (p * (dp - delta)).astype(BF16)
        probs[b, hg] = p.astype(BF16)

    def attend_block(b):
        for hg in range(NGROUP):
            attend(b, hg)

    attend_block(1)

    to_up.wait_recv()
    to_down.wait_recv()
    for copy in corners:
        copy.wait_recv()

    def project_caps(i, _):
        for part, out in ((1, k), (2, v)):
            r = dot(xc[...], w_cols(part, i), NN).astype(BF16)
            own = r[:128].reshape(4, 32, GROUP)
            rim = r[128:].reshape(8, 16, GROUP)
            for end in range(2):
                rows = slice(10 * end, 10 * end + 2)
                out[i, rows, 0:32] = own[2 * end : 2 * end + 2]
                out[i, rows, 32:48] = rim[2 * end : 2 * end + 2]
                out[i, rows, 48:64] = rim[4 + 2 * end : 6 + 2 * end]
        return 0

    lax.fori_loop(0, NGROUP, project_caps, 0)
    attend_block(0)
    attend_block(3)

    tensors = ((dscores, query_block), (probs, grad_block))

    def grad_caps(hg, _):
        for index, (weights, block) in enumerate(tensors):
            lanes = pl.ds(pl.multiple_of(index * CHAN + hg * GROUP, GROUP), GROUP)
            for end, b in ((0, 0), (1, 3)):
                r = dot(weights[b, hg, 256 * end : 256 * end + 128], block(b, hg), NN).astype(BF16)
                for dst, src, size in ((0, 0, 32), (32, 64, 32), (64, 32, 16), (80, 96, 16), (96, 48, 16), (112, 112, 16)):
                    grads_cap[128 * end + dst : 128 * end + dst + size, lanes] = r[src : src + size]
        return 0

    lax.fori_loop(0, NGROUP, grad_caps, 0)

    def back_caps(n, _):
        lanes = pl.ds(pl.multiple_of(n * GROUP, GROUP), GROUP)
        cap_send[:, lanes] = dot(grads_cap[...], w[lanes, CHAN:], NT).astype(BF16)
        return 0

    lax.fori_loop(0, NGROUP, back_caps, 0)
    back_up = send(cap_send.at[0:128], cap_recv.at[128:256], up)
    back_down = send(cap_send.at[128:256], cap_recv.at[0:128], down)

    attend_block(2)

    def window_sums(weights, block, hg, start, size):
        parts = []
        for b in range(BLOCKS):
            rows = weights[b, hg].reshape(6, 64, GROUP)[:, start : start + size].reshape(6 * size, GROUP)
            parts.append(dot(rows, block(b, hg), NN))
        sums = []
        for p in range(2, 10):
            terms = [parts[b][(p - 2 * b) * size : (p - 2 * b + 1) * size] for b in range(BLOCKS) if 0 <= p - 2 * b < 6]
            sums.append(sum(terms[1:], terms[0]))
        return sums

    def grad_sides(hg, _):
        for index, (weights, block) in enumerate(tensors):
            lanes = pl.ds(pl.multiple_of(index * CHAN + hg * GROUP, GROUP), GROUP)
            sums = window_sums(weights, block, hg, 32, 32)
            for slot, p in enumerate((0, 1, 6, 7, 2, 3, 4, 5)):
                r = sums[p].astype(BF16)
                grads_side[16 * slot : 16 * slot + 16, lanes] = r[:16]
                grads_side[128 + 16 * slot : 144 + 16 * slot, lanes] = r[16:]
        return 0

    lax.fori_loop(0, NGROUP, grad_sides, 0)

    def back_sides(n, _):
        lanes = pl.ds(pl.multiple_of(n * GROUP, GROUP), GROUP)
        r = dot(grads_side[...], w[lanes, CHAN:], NT)
        for side in range(2):
            side_edge[side, :, lanes] = r[128 * side : 128 * side + 64]
            side_send[side, 64:128, lanes] = r[128 * side + 64 : 128 * side + 128].astype(BF16)
        return 0

    lax.fori_loop(0, NGROUP, back_sides, 0)
    returns = [
        send(side_send.at[0, 64:128], side_recv.at[1, 64:128], left),
        send(side_send.at[1, 64:128], side_recv.at[0, 64:128], right),
    ]

    def grad_own(hg, _):
        for index, (weights, block) in enumerate(tensors):
            lanes = pl.ds(pl.multiple_of((1 + index) * CHAN + hg * GROUP, GROUP), GROUP)
            for p, r in enumerate(window_sums(weights, block, hg, 0, 32)):
                grads_own[32 * p : 32 * p + 32, lanes] = r.astype(BF16)
        return 0

    lax.fori_loop(0, NGROUP, grad_own, 0)

    def outputs(b, _):
        rows = pl.ds(64 * b, 64)
        for hg in range(NGROUP):
            lanes = slice(hg * GROUP, (hg + 1) * GROUP)
            keys = k[hg, pl.ds(2 * b, 6)].reshape(384, GROUP)
            vals = v[hg, pl.ds(2 * b, 6)].reshape(384, GROUP)
            att_ref[rows, lanes] = take_diagonal(dot(probs[b, hg], vals, TN)).astype(BF16)
            grads_own[rows, lanes] = (take_diagonal(dot(dscores[b, hg], keys, TN)) * 0.125).astype(BF16)
        return 0

    lax.fori_loop(0, 2, outputs, 0)

    back_up.wait_recv()
    back_down.wait_recv()
    for side in range(2):
        for end in range(2):
            rows = slice(32 * end, 32 * end + 32)
            rim = slice(128 * end + 64 + 32 * side, 128 * end + 96 + 32 * side)
            side_send[side, rows] = (side_edge[side, rows] + cap_recv[rim].astype(F32)).astype(BF16)
    returns.append(send(side_send.at[0, 0:64], side_recv.at[1, 0:64], left))
    returns.append(send(side_send.at[1, 0:64], side_recv.at[0, 0:64], right))

    lax.fori_loop(2, BLOCKS, outputs, 0)

    def back_own(n, _):
        lanes = pl.ds(pl.multiple_of(n * GROUP, GROUP), GROUP)
        r = dot(grads_own[...], w[lanes, :], NT)
        own_out[0:64, lanes] = r[:64] + cap_recv[0:64, lanes].astype(F32)
        own_out[64:192, lanes] = r[64:192]
        own_out[192:256, lanes] = r[192:] + cap_recv[128:192, lanes].astype(F32)
        return 0

    lax.fori_loop(0, NGROUP, back_own, 0)
    for copy in returns:
        copy.wait_recv()
    for slot, row in enumerate((0, 1, 2, 3, 12, 13, 14, 15, 4, 5, 6, 7, 8, 9, 10, 11)):
        both = jnp.concatenate([side_recv[side, 8 * slot : 8 * slot + 8].astype(F32) for side in range(2)], 0)
        rows = slice(16 * row, 16 * row + 16)
        fg_ref[rows] = (own_out[rows] + both).astype(BF16)

    for copy in sent:
        copy.wait_send()


def hand_over(att_ref, grad_ref, att_out, grad_out, held, in_sem, out_sem):
    parts = []
    for index, (src, dst) in enumerate(((att_ref, att_out), (grad_ref, grad_out))):
        for part in range(4):
            rows, slot = slice(64 * part, 64 * part + 64), 4 * index + part
            fetch = pltpu.make_async_copy(src.at[rows], held.at[slot], in_sem.at[slot])
            store = pltpu.make_async_copy(held.at[slot], dst.at[rows], out_sem.at[slot])
            fetch.start()
            parts.append((fetch, store))
    for fetch, store in parts:
        fetch.wait()
        store.start()
    for _, store in parts:
        store.wait()


def shards(features, w_qkv, cotangent, row_reach, col_reach):
    vmem = pl.BlockSpec(memory_space=pltpu.VMEM)
    smem = pl.BlockSpec(memory_space=pltpu.SMEM)
    any_space = pl.BlockSpec(memory_space=pl.ANY)
    flat = [jax.ShapeDtypeStruct((256, CHAN), BF16)] * 2
    att, grad = pl.pallas_call(
        kernel,
        out_shape=flat,
        in_specs=[any_space, any_space, any_space, smem, smem],
        out_specs=[vmem, vmem],
        scratch_shapes=[
            pltpu.VMEM((256, CHAN), BF16),
            pltpu.VMEM((256, CHAN), BF16),
            pltpu.VMEM((256, CHAN), BF16),
            pltpu.VMEM((2, 128, CHAN), BF16),
            pltpu.VMEM((CHAN, 3 * CHAN), BF16),
            pltpu.VMEM((16, 16, CHAN), BF16),
            pltpu.VMEM((NGROUP, 256, GROUP), BF16),
            pltpu.VMEM((NGROUP, 12, 64, GROUP), BF16),
            pltpu.VMEM((NGROUP, 12, 64, GROUP), BF16),
            pltpu.VMEM((BLOCKS, 384, 128), F32),
            pltpu.VMEM((BLOCKS, NGROUP, 384, GROUP), BF16),
            pltpu.VMEM((BLOCKS, NGROUP, 384, GROUP), BF16),
            pltpu.VMEM((256, 2 * CHAN), BF16),
            pltpu.VMEM((256, 2 * CHAN), BF16),
            pltpu.VMEM((256, 3 * CHAN), BF16),
            pltpu.VMEM((2, 64, CHAN), F32),
            pltpu.VMEM((256, CHAN), F32),
            pltpu.VMEM((256, CHAN), BF16),
            pltpu.VMEM((256, CHAN), BF16),
            pltpu.VMEM((2, 128, CHAN), BF16),
            pltpu.VMEM((2, 128, CHAN), BF16),
            pltpu.SemaphoreType.DMA((5,)),
            pltpu.SemaphoreType.DMA((14,)),
            pltpu.SemaphoreType.DMA((14,)),
        ],
        compiler_params=pltpu.CompilerParams(
            collective_id=0, has_side_effects=True, vmem_limit_bytes=56 << 20
        ),
        name="sphere_attention",
    )(features.reshape(256, CHAN), w_qkv, cotangent, row_reach, col_reach)
    att, grad = pl.pallas_call(
        hand_over,
        out_shape=flat,
        in_specs=[any_space, any_space],
        out_specs=[any_space, any_space],
        scratch_shapes=[
            pltpu.VMEM((8, 64, CHAN), BF16),
            pltpu.SemaphoreType.DMA((8,)),
            pltpu.SemaphoreType.DMA((8,)),
        ],
        name="hand_over",
    )(att, grad)
    return att.reshape(features.shape), grad.reshape(features.shape)


def solution(mesh):
    placed = (P("lat", "lon", None), P(), P("lat", "lon", None), P(), P())
    return jax.shard_map(
        shards,
        mesh=mesh,
        in_specs=placed,
        out_specs=(P("lat", "lon", None), P("lat", "lon", None)),
        check_vma=False,
    )
```

time: 56.6 us -> 48.2 us (0.85)
  Pallas kernels: 52 us -> 47.4 us
  local copies, waits for them, and re-layouts: 3.76 us -> 0 us
    pallas_call x1 -> x2, Pallas kernels: 52 us -> 47.4 us  [the longest x1 45.4 us: shards(): pl.pallas_call(kernel, out_shape=flat, in_specs=[any_space, any_space, an...]
    unnamed x2 -> x0, local copies, waits for them, and re-layouts: 3.76 us -> none
where the time goes in v2:
time: 48.2 us; the launch traced here: 48.1 us
  Pallas kernels  47.4 us (98%)
  between operations  0.64 us (1%)
    pallas_call x1, Pallas kernels, shards(): pl.pallas_call(kernel, out_shape=flat, in_specs=[any_space, any_space, an...  45.4 us
    pallas_call x1, Pallas kernels, shards(): pl.pallas_call(hand_over, out_shape=flat, in_specs=[any_space, any_space]...  2.09 us

profile of v2, /device:TPU:1, one launch (start us, length us, event | category | flops | bytes accessed | tf_op | source)
XLA Modules:
  0.0 48.1 jit_solution(13332753424292048047)
XLA Ops:
  0.6 45.4 %sphere_attention.1 = (bf16[256,1024]{1,0:T(8,128)(2,1)}, bf16[256,1024]{1,0:T(8,128)(2,1)}) custom-call(bf16[256,1024]{1,0:T(8,128)(2,1)} %bitcast.3, bf16[1024,3072]{1,0:T(8,128)(2,1)} %w_hbm.1, bf16[16,16,1024]{2,1,0:T(8,128)(2,1)} %g_hbm.1, s32[256]{0:T(256)} %rr_ref.1, s32[256]{0:T(256)} %cc_ref.1), custom_call_target="tpu_custom_call" | custom-call | tf_op jit(solution)/shard_map/sphere_attention/pallas_call | solution.py:338
  46.0 2.1 %hand_over.1 = (bf16[256,1024]{1,0:T(8,128)(2,1)}, bf16[256,1024]{1,0:T(8,128)(2,1)}) custom-call(bf16[256,1024]{1,0:T(8,128)(2,1)} %get-tuple-element.6.att_ref, bf16[256,1024]{1,0:T(8,128)(2,1)} %get-tuple-element.7.grad_ref), custom_call_target="tpu_custom_call" | custom-call | tf_op jit(solution)/shard_map/hand_over/pallas_call | solution.py:374

commit v3 on v2

--- a/solution.py
+++ b/solution.py
@@ -36,6 +36,18 @@
     for head in range(1, 4):
         out = jnp.where(cols == head, o[64 * head : 64 * head + 64], out)
     return out
+
+
+def looped(body, count, unroll):
+    def step(i, carry):
+        for j in range(unroll):
+            body(i * unroll + j, carry)
+        return carry
+
+    if unroll == count:
+        step(0, 0)
+    else:
+        lax.fori_loop(0, count // unroll, step, 0)
 
 
 def kernel(
@@ -131,10 +143,10 @@
         return 0
 
     w_copies[0].wait()
-    lax.fori_loop(0, NGROUP, project_query, 0)
+    looped(project_query, NGROUP, 4)
     w_copies[1].wait()
     w_copies[2].wait()
-    lax.fori_loop(0, NGROUP, project_own, 0)
+    looped(project_own, NGROUP, 4)
 
     to_left.wait_recv()
     to_right.wait_recv()
@@ -151,7 +163,7 @@
             out[i, 2:10, 48:64] = r[8:]
         return 0
 
-    lax.fori_loop(0, NGROUP, project_sides, 0)
+    looped(project_sides, NGROUP, 4)
     g_copy.wait()
 
     def query_block(b, hg):
@@ -196,7 +208,7 @@
                 out[i, rows, 48:64] = rim[4 + 2 * end : 6 + 2 * end]
         return 0
 
-    lax.fori_loop(0, NGROUP, project_caps, 0)
+    looped(project_caps, NGROUP, 4)
     attend_block(0)
     attend_block(3)
 
@@ -211,14 +223,14 @@
                     grads_cap[128 * end + dst : 128 * end + dst + size, lanes] = r[src : src + size]
         return 0
 
-    lax.fori_loop(0, NGROUP, grad_caps, 0)
+    looped(grad_caps, NGROUP, 4)
 
     def back_caps(n, _):
         lanes = pl.ds(pl.multiple_of(n * GROUP, GROUP), GROUP)
         cap_send[:, lanes] = dot(grads_cap[...], w[lanes, CHAN:], NT).astype(BF16)
         return 0
 
-    lax.fori_loop(0, NGROUP, back_caps, 0)
+    looped(back_caps, NGROUP, 4)
     back_up = send(cap_send.at[0:128], cap_recv.at[128:256], up)
     back_down = send(cap_send.at[128:256], cap_recv.at[0:128], down)
 
@@ -245,7 +257,7 @@
                 grads_side[128 + 16 * slot : 144 + 16 * slot, lanes] = r[16:]
         return 0
 
-    lax.fori_loop(0, NGROUP, grad_sides, 0)
+    looped(grad_sides, NGROUP, 4)
 
     def back_sides(n, _):
         lanes = pl.ds(pl.multiple_of(n * GROUP, GROUP), GROUP)
@@ -255,7 +267,7 @@
             side_send[side, 64:128, lanes] = r[128 * side + 64 : 128 * side + 128].astype(BF16)
         return 0
 
-    lax.fori_loop(0, NGROUP, back_sides, 0)
+    looped(back_sides, NGROUP, 4)
     returns = [
         send(side_send.at[0, 64:128], side_recv.at[1, 64:128], left),
         send(side_send.at[1, 64:128], side_recv.at[0, 64:128], right),
@@ -268,7 +280,7 @@
                 grads_own[32 * p : 32 * p + 32, lanes] = r.astype(BF16)
         return 0
 
-    lax.fori_loop(0, NGROUP, grad_own, 0)
+    looped(grad_own, NGROUP, 4)
 
     def outputs(b, _):
         rows = pl.ds(64 * b, 64)
@@ -302,7 +314,7 @@
         own_out[192:256, lanes] = r[192:] + cap_recv[128:192, lanes].astype(F32)
         return 0
 
-    lax.fori_loop(0, NGROUP, back_own, 0)
+    looped(back_own, NGROUP, 4)
     for copy in returns:
         copy.wait_recv()
     for slot, row in enumerate((0, 1, 2, 3, 12, 13, 14, 15, 4, 5, 6, 7, 8, 9, 10, 11)):

time: 48.2 us -> 45.5 us (0.944)
  the two profiles are of different devices: /device:TPU:1 before, /device:TPU:8 now
where the time goes in v3:
time: 45.5 us; the launch traced here: 45.4 us
  Pallas kernels  44.6 us (98%)
  between operations  0.8 us (2%)
    pallas_call x1, Pallas kernels, shards(): pl.pallas_call(kernel, out_shape=flat, in_specs=[any_space, any_space, an...  42.5 us
    pallas_call x1, Pallas kernels, shards(): pl.pallas_call(hand_over, out_shape=flat, in_specs=[any_space, any_space]...  2.09 us

profile of v3, /device:TPU:8, one launch (start us, length us, event | category | flops | bytes accessed | tf_op | source)
XLA Modules:
  0.0 45.4 jit_solution(6637242108395874392)
XLA Ops:
  0.6 42.5 %sphere_attention.1 = (bf16[256,1024]{1,0:T(8,128)(2,1)}, bf16[256,1024]{1,0:T(8,128)(2,1)}) custom-call(bf16[256,1024]{1,0:T(8,128)(2,1)} %bitcast.3, bf16[1024,3072]{1,0:T(8,128)(2,1)} %w_hbm.1, bf16[16,16,1024]{2,1,0:T(8,128)(2,1)} %g_hbm.1, s32[256]{0:T(256)} %rr_ref.1, s32[256]{0:T(256)} %cc_ref.1), custom_call_target="tpu_custom_call" | custom-call | tf_op jit(solution)/shard_map/sphere_attention/pallas_call | solution.py:350
  43.1 2.1 %hand_over.1 = (bf16[256,1024]{1,0:T(8,128)(2,1)}, bf16[256,1024]{1,0:T(8,128)(2,1)}) custom-call(bf16[256,1024]{1,0:T(8,128)(2,1)} %get-tuple-element.6.att_ref, bf16[256,1024]{1,0:T(8,128)(2,1)} %get-tuple-element.7.grad_ref), custom_call_target="tpu_custom_call" | custom-call | tf_op jit(solution)/shard_map/hand_over/pallas_call | solution.py:386

commit v4 on v3

--- a/solution.py
+++ b/solution.py
@@ -12,6 +12,7 @@
 GROUP = 256
 NGROUP = CHAN // GROUP
 BLOCKS = 4
+OUTER_FIRST = (0, 1, 2, 3, 12, 13, 14, 15, 4, 5, 6, 7, 8, 9, 10, 11)
 F32 = jnp.float32
 BF16 = jnp.bfloat16
 MESH = pl.DeviceIdType.MESH
@@ -51,10 +52,10 @@
 
 
 def kernel(
-    x_hbm, w_hbm, g_hbm, rr_ref, cc_ref, att_ref, fg_ref,
-    xm, xs, xc, edges, w, g, q, k, v, bias, probs, dscores,
+    x_hbm, w_hbm, g_hbm, rr_ref, cc_ref, att_out, grad_out,
+    xm, xh, edges, w, g, q, k, v, bias, probs, dscores,
     grads_cap, grads_side, grads_own, side_edge, own_out,
-    cap_send, cap_recv, side_send, side_recv,
+    cap_send, cap_recv, side_send, side_recv, att_ref, fg_ref,
     local_sem, send_sem, recv_sem,
 ):
     lat, lon = lax.axis_index("lat"), lax.axis_index("lon")
@@ -81,9 +82,9 @@
     g_copy = fetch(4, g_hbm, g)
 
     own_copy.wait()
-    for row in range(16):
-        edges[0, 8 * row : 8 * row + 8] = xm[16 * row : 16 * row + 8]
-        edges[1, 8 * row : 8 * row + 8] = xm[16 * row + 8 : 16 * row + 16]
+    for slot, row in enumerate(OUTER_FIRST):
+        edges[0, 8 * slot : 8 * slot + 8] = xm[16 * row : 16 * row + 8]
+        edges[1, 8 * slot : 8 * slot + 8] = xm[16 * row + 8 : 16 * row + 16]
     pl.semaphore_wait(barrier, 4)
 
     sent = []
@@ -102,10 +103,16 @@
         sent.append(copy)
         return copy
 
-    to_left = send(edges.at[0], xs.at[128:256], left)
-    to_right = send(edges.at[1], xs.at[0:128], right)
-    to_up = send(xm.at[0:64], xc.at[64:128], up)
-    to_down = send(xm.at[192:256], xc.at[0:64], down)
+    near = [
+        send(edges.at[0, 0:64], xh.at[64:128], left),
+        send(edges.at[1, 0:64], xh.at[0:64], right),
+        send(xm.at[0:64], xh.at[192:256], up),
+        send(xm.at[192:256], xh.at[128:192], down),
+    ]
+    far = [
+        send(edges.at[0, 64:128], xh.at[320:384], left),
+        send(edges.at[1, 64:128], xh.at[256:320], right),
+    ]
 
     first_row = lat * 16
     height = n_lat * 16
@@ -136,34 +143,51 @@
         q[i] = r.astype(BF16) * BF16(0.125)
         return 0
 
-    def project_own(i, _):
-        cells = xm[...]
-        k[i, 2:10, 0:32] = dot(cells, w_cols(1, i), NN).astype(BF16).reshape(8, 32, GROUP)
-        v[i, 2:10, 0:32] = dot(cells, w_cols(2, i), NN).astype(BF16).reshape(8, 32, GROUP)
-        return 0
+    def project_own(part, out):
+        def project(i, _):
+            r = dot(xm[...], w_cols(part, i), NN).astype(BF16)
+            out[i, 2:10, 0:32] = r.reshape(8, 32, GROUP)
+            return 0
+
+        looped(project, NGROUP, 4)
 
     w_copies[0].wait()
     looped(project_query, NGROUP, 4)
     w_copies[1].wait()
+    project_own(1, k)
+    for copy in near:
+        copy.wait_recv()
+    for side in range(2):
+        rows = 64 * side
+        far.append(send(xh.at[rows : rows + 32], xh.at[416 + rows : 448 + rows], up))
+        far.append(send(xh.at[rows + 32 : rows + 64], xh.at[384 + rows : 416 + rows], down))
     w_copies[2].wait()
-    looped(project_own, NGROUP, 4)
-
-    to_left.wait_recv()
-    to_right.wait_recv()
-    corners = []
-    for side in range(2):
-        base = 128 * side
-        corners.append(send(xs.at[base : base + 32], xc.at[160 + 64 * side : 192 + 64 * side], up))
-        corners.append(send(xs.at[base + 96 : base + 128], xc.at[128 + 64 * side : 160 + 64 * side], down))
-
-    def project_sides(i, _):
+    project_own(2, v)
+
+    def project_near(i, _):
         for part, out in ((1, k), (2, v)):
-            r = dot(xs[...], w_cols(part, i), NN).astype(BF16).reshape(16, 16, GROUP)
-            out[i, 2:10, 32:48] = r[:8]
-            out[i, 2:10, 48:64] = r[8:]
-        return 0
-
-    looped(project_sides, NGROUP, 4)
+            r = dot(xh[0:256], w_cols(part, i), NN).astype(BF16)
+            for end, rows in ((0, slice(2, 4)), (1, slice(8, 10))):
+                out[i, rows, 32:48] = r[32 * end : 32 * end + 32].reshape(2, 16, GROUP)
+                out[i, rows, 48:64] = r[64 + 32 * end : 96 + 32 * end].reshape(2, 16, GROUP)
+            out[i, 0:2, 0:32] = r[128:192].reshape(2, 32, GROUP)
+            out[i, 10:12, 0:32] = r[192:256].reshape(2, 32, GROUP)
+        return 0
+
+    def project_far(i, _):
+        for part, out in ((1, k), (2, v)):
+            r = dot(xh[256:512], w_cols(part, i), NN).astype(BF16)
+            out[i, 4:8, 32:48] = r[0:64].reshape(4, 16, GROUP)
+            out[i, 4:8, 48:64] = r[64:128].reshape(4, 16, GROUP)
+            for end, rows in ((0, slice(0, 2)), (1, slice(10, 12))):
+                out[i, rows, 32:48] = r[128 + 32 * end : 160 + 32 * end].reshape(2, 16, GROUP)
+                out[i, rows, 48:64] = r[192 + 32 * end : 224 + 32 * end].reshape(2, 16, GROUP)
+        return 0
+
+    looped(project_near, NGROUP, 4)
+    for copy in far:
+        copy.wait_recv()
+    looped(project_far, NGROUP, 4)
     g_copy.wait()
 
     def query_block(b, hg):
@@ -189,26 +213,6 @@
         for hg in range(NGROUP):
             attend(b, hg)
 
-    attend_block(1)
-
-    to_up.wait_recv()
-    to_down.wait_recv()
-    for copy in corners:
-        copy.wait_recv()
-
-    def project_caps(i, _):
-        for part, out in ((1, k), (2, v)):
-            r = dot(xc[...], w_cols(part, i), NN).astype(BF16)
-            own = r[:128].reshape(4, 32, GROUP)
-            rim = r[128:].reshape(8, 16, GROUP)
-            for end in range(2):
-                rows = slice(10 * end, 10 * end + 2)
-                out[i, rows, 0:32] = own[2 * end : 2 * end + 2]
-                out[i, rows, 32:48] = rim[2 * end : 2 * end + 2]
-                out[i, rows, 48:64] = rim[4 + 2 * end : 6 + 2 * end]
-        return 0
-
-    looped(project_caps, NGROUP, 4)
     attend_block(0)
     attend_block(3)
 
@@ -234,6 +238,7 @@
     back_up = send(cap_send.at[0:128], cap_recv.at[128:256], up)
     back_down = send(cap_send.at[128:256], cap_recv.at[0:128], down)
 
+    attend_block(1)
     attend_block(2)
 
     def window_sums(weights, block, hg, start, size):
@@ -292,7 +297,7 @@
             grads_own[rows, lanes] = (take_diagonal(dot(dscores[b, hg], keys, TN)) * 0.125).astype(BF16)
         return 0
 
-    lax.fori_loop(0, 2, outputs, 0)
+    outputs(0, 0)
 
     back_up.wait_recv()
     back_down.wait_recv()
@@ -304,7 +309,8 @@
     returns.append(send(side_send.at[0, 0:64], side_recv.at[1, 0:64], left))
     returns.append(send(side_send.at[1, 0:64], side_recv.at[0, 0:64], right))
 
-    lax.fori_loop(2, BLOCKS, outputs, 0)
+    lax.fori_loop(1, BLOCKS, outputs, 0)
+    stores = [fetch(5, att_ref, att_out)]
 
     def back_own(n, _):
         lanes = pl.ds(pl.multiple_of(n * GROUP, GROUP), GROUP)
@@ -315,13 +321,24 @@
         return 0
 
     looped(back_own, NGROUP, 4)
-    for copy in returns:
+
+    def finish(slots):
+        for slot in slots:
+            both = jnp.concatenate([side_recv[side, 8 * slot : 8 * slot + 8].astype(F32) for side in range(2)], 0)
+            rows = slice(16 * OUTER_FIRST[slot], 16 * OUTER_FIRST[slot] + 16)
+            fg_ref[rows] = (own_out[rows] + both).astype(BF16)
+
+    for copy in returns[:2]:
         copy.wait_recv()
-    for slot, row in enumerate((0, 1, 2, 3, 12, 13, 14, 15, 4, 5, 6, 7, 8, 9, 10, 11)):
-        both = jnp.concatenate([side_recv[side, 8 * slot : 8 * slot + 8].astype(F32) for side in range(2)], 0)
-        rows = slice(16 * row, 16 * row + 16)
-        fg_ref[rows] = (own_out[rows] + both).astype(BF16)
-
+    finish(range(8, 16))
+    stores.append(fetch(6, fg_ref.at[64:192], grad_out.at[64:192]))
+    for copy in returns[2:]:
+        copy.wait_recv()
+    finish(range(8))
+    stores.append(fetch(7, fg_ref.at[0:64], grad_out.at[0:64]))
+    stores.append(fetch(8, fg_ref.at[192:256], grad_out.at[192:256]))
+    for copy in stores:
+        copy.wait()
     for copy in sent:
         copy.wait_send()
 
@@ -343,7 +360,6 @@
 
 
 def shards(features, w_qkv, cotangent, row_reach, col_reach):
-    vmem = pl.BlockSpec(memory_space=pltpu.VMEM)
     smem = pl.BlockSpec(memory_space=pltpu.SMEM)
     any_space = pl.BlockSpec(memory_space=pl.ANY)
     flat = [jax.ShapeDtypeStruct((256, CHAN), BF16)] * 2
@@ -351,11 +367,10 @@
         kernel,
         out_shape=flat,
         in_specs=[any_space, any_space, any_space, smem, smem],
-        out_specs=[vmem, vmem],
+        out_specs=[any_space, any_space],
         scratch_shapes=[
             pltpu.VMEM((256, CHAN), BF16),
-            pltpu.VMEM((256, CHAN), BF16),
-            pltpu.VMEM((256, CHAN), BF16),
+            pltpu.VMEM((512, CHAN), BF16),
             pltpu.VMEM((2, 128, CHAN), BF16),
             pltpu.VMEM((CHAN, 3 * CHAN), BF16),
             pltpu.VMEM((16, 16, CHAN), BF16),
@@ -374,9 +389,11 @@
             pltpu.VMEM((256, CHAN), BF16),
             pltpu.VMEM((2, 128, CHAN), BF16),
             pltpu.VMEM((2, 128, CHAN), BF16),
-            pltpu.SemaphoreType.DMA((5,)),
-            pltpu.SemaphoreType.DMA((14,)),
-            pltpu.SemaphoreType.DMA((14,)),
+            pltpu.VMEM((256, CHAN), BF16),
+            pltpu.VMEM((256, CHAN), BF16),
+            pltpu.SemaphoreType.DMA((9,)),
+            pltpu.SemaphoreType.DMA((16,)),
+            pltpu.SemaphoreType.DMA((16,)),
         ],
         compiler_params=pltpu.CompilerParams(
             collective_id=0, has_side_effects=True, vmem_limit_bytes=56 << 20

time: 45.5 us -> 44.5 us (0.978)
  Pallas kernels: 44.6 us -> 43.6 us
    pallas_call x1, Pallas kernels: 42.5 us -> 41.5 us  [shards(): pl.pallas_call(kernel, out_shape=flat, in_specs=[any_space, any_space, an...]
where the time goes in v4:
time: 44.5 us; the launch traced here: 44.4 us
  Pallas kernels  43.6 us (98%)
  between operations  0.8 us (2%)
    pallas_call x1, Pallas kernels, shards(): pl.pallas_call(kernel, out_shape=flat, in_specs=[any_space, any_space, an...  41.5 us
    pallas_call x1, Pallas kernels, shards(): pl.pallas_call(hand_over, out_shape=flat, in_specs=[any_space, any_space]...  2.09 us

profile of v4, /device:TPU:8, one launch (start us, length us, event | category | flops | bytes accessed | tf_op | source)
XLA Modules:
  0.0 44.4 jit_solution(3124312347547947771)
XLA Ops:
  0.6 41.5 %sphere_attention.1 = (bf16[256,1024]{1,0:T(8,128)(2,1)}, bf16[256,1024]{1,0:T(8,128)(2,1)}) custom-call(bf16[256,1024]{1,0:T(8,128)(2,1)} %bitcast.3, bf16[1024,3072]{1,0:T(8,128)(2,1)} %w_hbm.1, bf16[16,16,1024]{2,1,0:T(8,128)(2,1)} %g_hbm.1, s32[256]{0:T(256)} %rr_ref.1, s32[256]{0:T(256)} %cc_ref.1), custom_call_target="tpu_custom_call" | custom-call | tf_op jit(solution)/shard_map/sphere_attention/pallas_call | solution.py:366
  42.1 2.1 %hand_over.1 = (bf16[256,1024]{1,0:T(8,128)(2,1)}, bf16[256,1024]{1,0:T(8,128)(2,1)}) custom-call(bf16[256,1024]{1,0:T(8,128)(2,1)} %get-tuple-element.6.att_ref, bf16[256,1024]{1,0:T(8,128)(2,1)} %get-tuple-element.7.grad_ref), custom_call_target="tpu_custom_call" | custom-call | tf_op jit(solution)/shard_map/hand_over/pallas_call | solution.py:403

commit v5 on v4

--- a/solution.py
+++ b/solution.py
@@ -53,7 +53,7 @@
 
 def kernel(
     x_hbm, w_hbm, g_hbm, rr_ref, cc_ref, att_out, grad_out,
-    xm, xh, edges, w, g, q, k, v, bias, probs, dscores,
+    xm, xh, edges, w, g, q, q_diag, g_diag, k, v, bias, probs, dscores,
     grads_cap, grads_side, grads_own, side_edge, own_out,
     cap_send, cap_recv, side_send, side_recv, att_ref, fg_ref,
     local_sem, send_sem, recv_sem,
@@ -185,17 +185,24 @@
         return 0
 
     looped(project_near, NGROUP, 4)
+    g_copy.wait()
+
+    def lay_blocks(b, _):
+        for hg in range(NGROUP):
+            lanes = slice(hg * GROUP, (hg + 1) * GROUP)
+            q_diag[b, hg] = block_diagonal(q[hg, pl.ds(64 * b, 64)])
+            g_diag[b, hg] = block_diagonal(g[pl.ds(4 * b, 4), :, lanes].reshape(64, GROUP))
+        return 0
+
+    lax.fori_loop(0, BLOCKS, lay_blocks, 0)
     for copy in far:
         copy.wait_recv()
     looped(project_far, NGROUP, 4)
-    g_copy.wait()
-
     def query_block(b, hg):
-        return block_diagonal(q[hg, pl.ds(64 * b, 64)])
+        return q_diag[b, hg]
 
     def grad_block(b, hg):
-        lanes = slice(hg * GROUP, (hg + 1) * GROUP) if isinstance(hg, int) else pl.ds(pl.multiple_of(hg * GROUP, GROUP), GROUP)
-        return block_diagonal(g[pl.ds(4 * b, 4), :, lanes].reshape(64, GROUP))
+        return g_diag[b, hg]
 
     def attend(b, hg):
         keys = k[hg, pl.ds(2 * b, 6)].reshape(384, GROUP)
@@ -297,7 +304,6 @@
             grads_own[rows, lanes] = (take_diagonal(dot(dscores[b, hg], keys, TN)) * 0.125).astype(BF16)
         return 0
 
-    outputs(0, 0)
 
     back_up.wait_recv()
     back_down.wait_recv()
@@ -309,7 +315,7 @@
     returns.append(send(side_send.at[0, 0:64], side_recv.at[1, 0:64], left))
     returns.append(send(side_send.at[1, 0:64], side_recv.at[0, 0:64], right))
 
-    lax.fori_loop(1, BLOCKS, outputs, 0)
+    lax.fori_loop(0, BLOCKS, outputs, 0)
     stores = [fetch(5, att_ref, att_out)]
 
     def back_own(n, _):
@@ -375,6 +381,8 @@
             pltpu.VMEM((CHAN, 3 * CHAN), BF16),
             pltpu.VMEM((16, 16, CHAN), BF16),
             pltpu.VMEM((NGROUP, 256, GROUP), BF16),
+            pltpu.VMEM((BLOCKS, NGROUP, 256, GROUP), BF16),
+            pltpu.VMEM((BLOCKS, NGROUP, 256, GROUP), BF16),
             pltpu.VMEM((NGROUP, 12, 64, GROUP), BF16),
             pltpu.VMEM((NGROUP, 12, 64, GROUP), BF16),
             pltpu.VMEM((BLOCKS, 384, 128), F32),

time: 44.5 us -> 44.3 us (level)
  no operation moved by 1% of the time
where the time goes in v5:
time: 44.3 us; the launch traced here: 44.1 us
  Pallas kernels  43.3 us (98%)
  between operations  0.8 us (2%)
    pallas_call x1, Pallas kernels, shards(): pl.pallas_call(kernel, out_shape=flat, in_specs=[any_space, any_space, an...  41.3 us
    pallas_call x1, Pallas kernels, shards(): pl.pallas_call(hand_over, out_shape=flat, in_specs=[any_space, any_space]...  2.09 us

profile of v5, /device:TPU:8, one launch (start us, length us, event | category | flops | bytes accessed | tf_op | source)
XLA Modules:
  0.0 44.1 jit_solution(5423851896995479242)
XLA Ops:
  0.6 41.3 %sphere_attention.1 = (bf16[256,1024]{1,0:T(8,128)(2,1)}, bf16[256,1024]{1,0:T(8,128)(2,1)}) custom-call(bf16[256,1024]{1,0:T(8,128)(2,1)} %bitcast.3, bf16[1024,3072]{1,0:T(8,128)(2,1)} %w_hbm.1, bf16[16,16,1024]{2,1,0:T(8,128)(2,1)} %g_hbm.1, s32[256]{0:T(256)} %rr_ref.1, s32[256]{0:T(256)} %cc_ref.1), custom_call_target="tpu_custom_call" | custom-call | tf_op jit(solution)/shard_map/sphere_attention/pallas_call | solution.py:372
  41.9 2.1 %hand_over.1 = (bf16[256,1024]{1,0:T(8,128)(2,1)}, bf16[256,1024]{1,0:T(8,128)(2,1)}) custom-call(bf16[256,1024]{1,0:T(8,128)(2,1)} %get-tuple-element.6.att_ref, bf16[256,1024]{1,0:T(8,128)(2,1)} %get-tuple-element.7.grad_ref), custom_call_target="tpu_custom_call" | custom-call | tf_op jit(solution)/shard_map/hand_over/pallas_call | solution.py:411

commit v6 on v5

--- a/solution.py
+++ b/solution.py
@@ -249,14 +249,15 @@
     attend_block(2)
 
     def window_sums(weights, block, hg, start, size):
-        parts = []
+        sums = [None] * 8
         for b in range(BLOCKS):
-            rows = weights[b, hg].reshape(6, 64, GROUP)[:, start : start + size].reshape(6 * size, GROUP)
-            parts.append(dot(rows, block(b, hg), NN))
-        sums = []
-        for p in range(2, 10):
-            terms = [parts[b][(p - 2 * b) * size : (p - 2 * b + 1) * size] for b in range(BLOCKS) if 0 <= p - 2 * b < 6]
-            sums.append(sum(terms[1:], terms[0]))
+            first, last = max(2 - 2 * b, 0), min(10 - 2 * b, 6)
+            rows = weights[b, hg].reshape(6, 64, GROUP)[first:last, start : start + size]
+            r = dot(rows.reshape((last - first) * size, GROUP), block(b, hg), NN)
+            for p in range(first, last):
+                term = r[(p - first) * size : (p - first + 1) * size]
+                slot = p + 2 * b - 2
+                sums[slot] = term if sums[slot] is None else sums[slot] + term
         return sums
 
     def grad_sides(hg, _):

time: 44.3 us -> 44.3 us (level)
  no operation moved by 1% of the time
where the time goes in v6:
time: 44.3 us; the launch traced here: 44.1 us
  Pallas kernels  43.3 us (98%)
  between operations  0.8 us (2%)
    pallas_call x1, Pallas kernels, shards(): pl.pallas_call(kernel, out_shape=flat, in_specs=[any_space, any_space, an...  41.3 us
    pallas_call x1, Pallas kernels, shards(): pl.pallas_call(hand_over, out_shape=flat, in_specs=[any_space, any_space]...  2.09 us

profile of v6, /device:TPU:8, one launch (start us, length us, event | category | flops | bytes accessed | tf_op | source)
XLA Modules:
  0.0 44.1 jit_solution(4831503031864040567)
XLA Ops:
  0.6 41.3 %sphere_attention.1 = (bf16[256,1024]{1,0:T(8,128)(2,1)}, bf16[256,1024]{1,0:T(8,128)(2,1)}) custom-call(bf16[256,1024]{1,0:T(8,128)(2,1)} %bitcast.3, bf16[1024,3072]{1,0:T(8,128)(2,1)} %w_hbm.1, bf16[16,16,1024]{2,1,0:T(8,128)(2,1)} %g_hbm.1, s32[256]{0:T(256)} %rr_ref.1, s32[256]{0:T(256)} %cc_ref.1), custom_call_target="tpu_custom_call" | custom-call | tf_op jit(solution)/shard_map/sphere_attention/pallas_call | solution.py:373
  41.9 2.1 %hand_over.1 = (bf16[256,1024]{1,0:T(8,128)(2,1)}, bf16[256,1024]{1,0:T(8,128)(2,1)}) custom-call(bf16[256,1024]{1,0:T(8,128)(2,1)} %get-tuple-element.6.att_ref, bf16[256,1024]{1,0:T(8,128)(2,1)} %get-tuple-element.7.grad_ref), custom_call_target="tpu_custom_call" | custom-call | tf_op jit(solution)/shard_map/hand_over/pallas_call | solution.py:412
